TPU v7x, 32 devices: a whole 2x2x4 slice. The times are simulated.
32 devices in a mesh: dp: 8 (over y, x, core), mp: 4 (over z).
Axes of the slice: x: 2, y: 2, z: 4, core: 2. Of those that a mesh axis runs over, the one named last changes fastest.
Arguments:
- tokens: bfloat16 [12288, 768], P('dp'), may hold values from -6 to 6
- segment_ids: int32 [24, 512], P('dp'), may hold values from 0 to 3, never falling along the last dimension, each value on 1 to 256 neighbouring positions
- lengths: int32 [24], P('dp'), may hold values from 256 to 512, as said below
- cotangent: float32 [12288], P('dp'), may hold values from -6 to 6
- w_qkv: bfloat16 [768, 3, 768], P(None, None, 'mp'), may hold values from -0.21875 to 0.21875
- b_qv: bfloat16 [2, 768], P(None, 'mp'), may hold values from -3 to 3
- w_out: bfloat16 [768, 768], P('mp'), may hold values from -1.25 to 1.25
- b_out: bfloat16 [768], replicated, may hold values from -3 to 3
- gain_one: bfloat16 [768], replicated, may hold values from 0.5 to 1.5
- shift_one: bfloat16 [768], replicated, may hold values from -1.75 to 1.75
- w_up: bfloat16 [768, 3072], P(None, 'mp'), may hold values from -0.21875 to 0.21875
- b_up: bfloat16 [3072], P('mp'), may hold values from -3 to 3
- w_down: bfloat16 [3072, 768], P('mp'), may hold values from -0.15625 to 0.15625
- b_down: bfloat16 [768], replicated, may hold values from -3 to 3
- gain_two: bfloat16 [768], replicated, may hold values from 0.5 to 1.5
- w_head: bfloat16 [768], replicated, may hold values from -0.21875 to 0.21875
- b_head: bfloat16 [1], replicated, may hold values from -6 to 6
Outputs:
- token_weight: float32 [12288], P('dp')
- input_grad: float32 [12288, 768], P('dp')
- grad_qkv: float32 [768, 3, 768], P(None, None, 'mp')
- grad_qv_bias: float32 [2, 768], P(None, 'mp')
- grad_out: float32 [768, 768], P('mp')
- grad_out_bias: float32 [768], replicated
- grad_gain_one: float32 [768], replicated
- grad_shift_one: float32 [768], replicated
- grad_up: float32 [768, 3072], P(None, 'mp')
- grad_up_bias: float32 [3072], P('mp')
- grad_down: float32 [3072, 768], P('mp')
- grad_down_bias: float32 [768], replicated
- grad_gain_two: float32 [768], replicated
- grad_head: float32 [768], replicated
- grad_head_bias: float32 [1], replicated
Inputs may be any that keep to these rules, and one draw needn't show every extreme that they name: `lengths`: one packed row of each draw is full and one holds 256 tokens before its padding. `segment_ids`: non-decreasing along each packed row.
All inputs are finite; a program needn't handle non-finite values.
Results may differ from a plain program's by a relative error of at most 0.015.
Values sent between devices are 32-bit elements; how exact they have to be, the bound alone decides.
No kernel may reach another device: no remote copies, remote signals or barrier semaphores. Data moves between devices by JAX's collectives and lax.ppermute only.
A program may use at most 128 MiB of HBM per device.

v0:
```python
import jax
import jax.numpy as jnp
from jax import lax
from jax.sharding import PartitionSpec as P

HEAD = 64


norm_eps = 1e-12
highest = lax.Precision.HIGHEST


def layer_norm(residual, gain_vec, shift_vec):
    row_mean = jnp.mean(residual, axis=-1, keepdims=True)
    centered = residual - row_mean
    inv_std = lax.rsqrt(jnp.mean(centered * centered, axis=-1, keepdims=True) + norm_eps)
    normed = centered * inv_std
    return (normed * gain_vec + shift_vec, normed, inv_std)


def norm_back(grad_rows, normed, inv_std, gain_vec):
    grad_normed = grad_rows * gain_vec
    grad_res = (
        grad_normed
        - jnp.mean(grad_normed, axis=-1, keepdims=True)
        - normed * jnp.mean(grad_normed * normed, axis=-1, keepdims=True)
    ) * inv_std
    return (grad_res, jnp.sum(grad_rows * normed, axis=0), jnp.sum(grad_rows, axis=0))


def gelu_exact(values_in):
    return 0.5 * values_in * (1.0 + lax.erf(values_in * 0.7071067811865476))


def gelu_slope(values_in):
    return (
        0.5 * (1.0 + lax.erf(values_in * 0.7071067811865476))
        + values_in * jnp.exp(-0.5 * values_in * values_in) * 0.3989422804014327
    )


def contract_rows(left, right):
    return lax.dot_general(
        left, right, (((0,), (0,)), ((), ())), preferred_element_type=jnp.float32
    )


def contract_cols(left, right):
    return lax.dot_general(
        left, right, (((1,), (1,)), ((), ())), preferred_element_type=jnp.float32
    )


def token_head(norm_rows, head_vec, head_bias, valid_rows):
    logit_rows = jnp.dot(norm_rows, head_vec, precision=highest) + head_bias[0]
    return (logit_rows, jax.nn.softplus(logit_rows) * valid_rows)


def body(
    tokens,
    segment_ids,
    lengths,
    cotangent,
    w_qkv,
    b_qv,
    w_out,
    b_out,
    gain_one,
    shift_one,
    w_up,
    b_up,
    w_down,
    b_down,
    gain_two,
    w_head,
    b_head,
):
    row_count, seq_len = segment_ids.shape
    token_count = tokens.shape[0]
    local_width = w_qkv.shape[2]
    head_count = local_width // HEAD
    score_scale = HEAD ** (-0.5)
    b_qv_f = b_qv.astype(jnp.float32)
    b_out_f = b_out.astype(jnp.float32)
    gain_one_f = gain_one.astype(jnp.float32)
    shift_one_f = shift_one.astype(jnp.float32)
    b_up_f = b_up.astype(jnp.float32)
    b_down_f = b_down.astype(jnp.float32)
    gain_two_f = gain_two.astype(jnp.float32)
    w_head_f = w_head.astype(jnp.float32)
    b_head_f = b_head.astype(jnp.float32)
    positions = jnp.arange(seq_len)
    valid_mask = (positions[None, :] < lengths[:, None]).reshape(token_count).astype(jnp.float32)
    allowed = (segment_ids[:, :, None] == segment_ids[:, None, :]) & (
        (positions[None, None, :] < lengths[:, None, None])
        | (positions[None, :, None] == positions[None, None, :])
    )
    allowed = allowed[:, None]
    projected = jnp.einsum("td,dcn->tcn", tokens, w_qkv, preferred_element_type=jnp.float32)
    row_shape = (row_count, seq_len, head_count, HEAD)
    query_rows = (projected[:, 0] + b_qv_f[0]).astype(jnp.bfloat16).reshape(row_shape)
    key_rows = projected[:, 1].astype(jnp.bfloat16).reshape(row_shape)
    value_rows = (projected[:, 2] + b_qv_f[1]).astype(jnp.bfloat16).reshape(row_shape)
    scores = (
        jnp.einsum("rqhe,rkhe->rhqk", query_rows, key_rows, preferred_element_type=jnp.float32)
        * score_scale
    )
    scores = jnp.where(allowed, scores, -1e30)
    row_max = jnp.max(scores, axis=-1, keepdims=True)
    exponent = jnp.exp(scores - row_max)
    row_total = jnp.sum(exponent, axis=-1, keepdims=True)
    attn_weights = (exponent / row_total).astype(jnp.bfloat16)
    log_total = row_max + jnp.log(row_total)
    context = jnp.einsum(
        "rhqk,rkhe->rqhe", attn_weights, value_rows, preferred_element_type=jnp.float32
    )
    context_low = context.reshape(token_count, local_width).astype(jnp.bfloat16)
    partial_out = jnp.dot(context_low, w_out, preferred_element_type=jnp.float32)
    attn_total = lax.psum(partial_out, "mp")
    norm_one, normed_one, inv_one = layer_norm(
        tokens.astype(jnp.float32) + attn_total + b_out_f, gain_one_f, shift_one_f
    )
    norm_one_low = norm_one.astype(jnp.bfloat16)
    hidden_pre = jnp.dot(norm_one_low, w_up, preferred_element_type=jnp.float32) + b_up_f
    act_low = gelu_exact(hidden_pre).astype(jnp.bfloat16)
    partial_down = jnp.dot(act_low, w_down, preferred_element_type=jnp.float32)
    down_total = lax.psum(partial_down, "mp")
    norm_two, normed_two, inv_two = layer_norm(norm_one + down_total + b_down_f, gain_two_f, 0.0)
    logits, token_weight = token_head(norm_two, w_head_f, b_head_f, valid_mask)
    d_logits = cotangent * valid_mask * jax.nn.sigmoid(logits)
    grad_head = jnp.dot(d_logits, norm_two, precision=highest)
    grad_head_bias = jnp.sum(d_logits)[None]
    d_norm_two = d_logits[:, None] * w_head_f
    d_res_two, grad_gain_two, unused_shift = norm_back(d_norm_two, normed_two, inv_two, gain_two_f)
    grad_down_bias = jnp.sum(d_res_two, axis=0)
    d_res_two_low = d_res_two.astype(jnp.bfloat16)
    grad_down = contract_rows(act_low, d_res_two_low)
    d_hidden = contract_cols(d_res_two_low, w_down) * gelu_slope(hidden_pre)
    grad_up_bias = jnp.sum(d_hidden, axis=0)
    d_hidden_low = d_hidden.astype(jnp.bfloat16)
    grad_up = contract_rows(norm_one_low, d_hidden_low)
    up_part = contract_cols(d_hidden_low, w_up)
    d_norm_one = d_res_two + lax.psum(up_part, "mp")
    d_res_one, grad_gain_one, grad_shift_one = norm_back(
        d_norm_one, normed_one, inv_one, gain_one_f
    )
    grad_out_bias = jnp.sum(d_res_one, axis=0)
    d_res_one_low = d_res_one.astype(jnp.bfloat16)
    grad_out = contract_rows(context_low, d_res_one_low)
    d_context = contract_cols(d_res_one_low, w_out).astype(jnp.bfloat16).reshape(row_shape)
    scores_again = (
        jnp.einsum("rqhe,rkhe->rhqk", query_rows, key_rows, preferred_element_type=jnp.float32)
        * score_scale
    )
    scores_again = jnp.where(allowed, scores_again, -1e30)
    probs_again = jnp.exp(scores_again - log_total)
    grad_values = jnp.einsum(
        "rhqk,rqhe->rkhe",
        probs_again.astype(jnp.bfloat16),
        d_context,
        preferred_element_type=jnp.float32,
    )
    d_probs = jnp.einsum(
        "rqhe,rkhe->rhqk", d_context, value_rows, preferred_element_type=jnp.float32
    )
    d_scores = probs_again * (d_probs - jnp.sum(d_probs * probs_again, axis=-1, keepdims=True))
    d_scores_low = d_scores.astype(jnp.bfloat16)
    grad_queries = (
        jnp.einsum("rhqk,rkhe->rqhe", d_scores_low, key_rows, preferred_element_type=jnp.float32)
        * score_scale
    )
    grad_keys = (
        jnp.einsum("rhqk,rqhe->rkhe", d_scores_low, query_rows, preferred_element_type=jnp.float32)
        * score_scale
    )
    stacked_low = jnp.stack(
        (
            grad_queries.reshape(token_count, local_width),
            grad_keys.reshape(token_count, local_width),
            grad_values.reshape(token_count, local_width),
        ),
        axis=1,
    ).astype(jnp.bfloat16)
    grad_qv_bias = jnp.stack(
        (
            jnp.sum(stacked_low[:, 0].astype(jnp.float32), axis=0),
            jnp.sum(stacked_low[:, 2].astype(jnp.float32), axis=0),
        )
    )
    grad_qkv = jnp.einsum("td,tcn->dcn", tokens, stacked_low, preferred_element_type=jnp.float32)
    token_part = jnp.einsum("tcn,dcn->td", stacked_low, w_qkv, preferred_element_type=jnp.float32)
    input_grad = d_res_one + lax.psum(token_part, "mp")
    (
        grad_qkv,
        grad_qv_bias,
        grad_out,
        grad_out_bias,
        grad_gain_one,
        grad_shift_one,
        grad_up,
        grad_up_bias,
        grad_down,
        grad_down_bias,
        grad_gain_two,
        grad_head,
        grad_head_bias,
    ) = lax.psum(
        (
            grad_qkv,
            grad_qv_bias,
            grad_out,
            grad_out_bias,
            grad_gain_one,
            grad_shift_one,
            grad_up,
            grad_up_bias,
            grad_down,
            grad_down_bias,
            grad_gain_two,
            grad_head,
            grad_head_bias,
        ),
        "dp",
    )
    return (
        token_weight,
        input_grad,
        grad_qkv,
        grad_qv_bias,
        grad_out,
        grad_out_bias,
        grad_gain_one,
        grad_shift_one,
        grad_up,
        grad_up_bias,
        grad_down,
        grad_down_bias,
        grad_gain_two,
        grad_head,
        grad_head_bias,
    )


def solution(mesh):
    placed = (
        P("dp", None),
        P("dp", None),
        P("dp"),
        P("dp"),
        P(None, None, "mp"),
        P(None, "mp"),
        P("mp", None),
        P(),
        P(),
        P(),
        P(None, "mp"),
        P("mp"),
        P("mp", None),
        P(),
        P(),
        P(),
        P(),
    )
    return jax.shard_map(
        body,
        mesh=mesh,
        in_specs=placed,
        out_specs=(
            P("dp"),
            P("dp", None),
            P(None, None, "mp"),
            P(None, "mp"),
            P("mp", None),
            P(),
            P(),
            P(),
            P(None, "mp"),
            P("mp"),
            P("mp", None),
            P(),
            P(),
            P(),
            P(),
        ),
        check_vma=False,
    )
```

profile of v0, /device:TPU:0, one launch (start us, length us, event | category | flops | bytes accessed | tf_op | source)
XLA Modules:
  0.0 949.0 jit_solution(12910349751285489955)
XLA Ops:
  7.3 3.5 fusion.83
  35.3 174.1 %all-reduce.8.cloned.1.call-done = f32[1536,768]{1,0:T(8,128)} async-done(((f32[1536,768]{1,0:T(8,128)}), f32[1536,768]{1,0:T(8,128)}) %all-reduce.8.cloned.1.call-update) | async-done | bytes 4718608 | tf_op jit(solution)/shard_map/psum | solution.py:119
  209.4 3.8 fusion.77
  213.9 4.6 multiply_convert_fusion.1
  219.9 4.2 fusion.85
  225.5 169.7 %all-reduce.10.cloned.1.call-done = f32[1536,768]{1,0:T(8,128)} async-done(((f32[1536,768]{1,0:T(8,128)}), f32[1536,768]{1,0:T(8,128)}) %all-reduce.10.cloned.1.call-update) | async-done | bytes 4718608 | tf_op jit(solution)/shard_map/psum | solution.py:127
  395.2 4.7 fusion.76
  409.5 3.6 fusion.80
  414.4 4.3 fusion.51
  419.2 170.6 %all-reduce.12.cloned.1.call-done = f32[1536,768]{1,0:T(8,128)} async-done(((f32[1536,768]{1,0:T(8,128)}), f32[1536,768]{1,0:T(8,128)}) %all-reduce.12.cloned.1.call-update) | async-done | bytes 4718608 | tf_op jit(solution)/shard_map/psum | solution.py:143
  589.8 6.5 multiply_reduce_fusion.1
  596.4 4.0 fusion.75
  604.0 6.1 fusion.41
  610.1 7.1 multiply_reduce_fusion
  617.2 11.2 %multiply_convert_fusion = bf16[3,3,512,512]{2,3,1,0:T(8,128)(2,1)} fusion(f32[3,3,512,512]{2,3,1,0:T(8,128)} %get-tuple-element.56, f32[3,3,512,512]{2,3,1,0:T(8,128)} %copy-done.3, f32[3,3,512]{2,1,0:T(4,128)S(1)} %get-tuple-element.55, f32[3,3,512]{2,1,0:T(4,128)S(1)} %log_add_fusion), kind=kLoop, calls=%fused_computation | loop fusion | flops 9437184 | bytes 23629824 | tf_op jit(solution)/shard_map/convert_element_type | solution.py:167
  628.4 4.0 fusion.44
  640.8 5.4 convolution_bitcast_fusion
  646.3 6.7 fusion.53
  653.0 6.4 fusion.49
  664.6 5.2 fusion.59
  670.1 26.2 %all-reduce = (f32[2,192]{1,0:T(2,128)}, f32[768]{0:T(1024)}, f32[768]{0:T(1024)}, f32[768]{0:T(1024)}, f32[768]{0:T(1024)}, /*index=5*/f32[768]{0:T(1024)}, f32[768]{0:T(1024)}, f32[768]{0:T(1024)}, f32[1]{0:T(128)}) all-reduce(f32[2,192]{1,0:T(2,128)S(1)} %pad_maximum_fusion, ...), channel_id=1, replica_groups=mesh['dp'=8,'mp'=4] {'dp'}, use_global_device_ids=true, to_apply=%region_18.19 | all-reduce | flops 5761 | bytes 46088 | tf_op jit(solution)/shard_map/psum | solution.py:207
  696.3 121.0 %all-reduce.14.cloned.1.call-done = f32[1536,768]{1,0:T(8,128)} async-done(((f32[1536,768]{1,0:T(8,128)}), f32[1536,768]{1,0:T(8,128)}) %all-reduce.14.cloned.1.call-update) | async-done | bytes 4718608 | tf_op jit(solution)/shard_map/psum | solution.py:192
  817.3 6.6 add.170
  823.9 110.6 %all-reduce.16.cloned.1.call-done = (f32[768,3,192]{0,2,1:T(8,128)}, f32[192,768]{1,0:T(8,128)}, f32[768,768]{1,0:T(8,128)}, f32[768,768]{1,0:T(8,128)}) async-done(((f32[768,3,192]{0,2,1:T(8,128)}, f32[192,768]{1,0:T(8,128)}, f32[768,768]{1,0:T(8,128)}, f32[768,768]{1,0:T(8,128)}), (f32[768,3,192]{0,2,1:T(8,128)}, f32[192,768]{1,0:T(8,128)}, f32[768,768]{1,0:T(8,128)}, ...) | async-done | bytes 7077904 | tf_op jit(solution)/shard_map/psum | solution.py:207
  (153 shorter events, 63.6 us)
Async XLA Ops:
  7.2 206.7 %copy-start = (bf16[768,768]{1,0:T(8,128)(2,1)S(1)}, bf16[768,768]{1,0:T(8,128)(2,1)}, u32[]{:S(2)}) copy-start(bf16[768,768]{1,0:T(8,128)(2,1)} %param.27) | copy-start | bytes 3538948
  7.2 202.2 %all-reduce.8.cloned.1.call-start = ((), (), s32[]{:S(2)}) async-start(), calls=%async_computation | async-start | bytes 9437184 | tf_op jit(solution)/shard_map/psum | solution.py:119
  13.9 7.2 copy-start.18
  19.1 7.6 copy-start.9
  25.3 3.6 copy-start.3
  34.6 360.6 %all-reduce.10.cloned.1.call-start = ((), (), s32[]{:S(2)}) async-start(), calls=%async_computation.1 | async-start | bytes 9437184 | tf_op jit(solution)/shard_map/psum | solution.py:127
  213.2 5.3 copy-start.4
  213.9 6.0 copy-start.29
  224.1 365.7 %all-reduce.12.cloned.1.call-start = ((), (), s32[]{:S(2)}) async-start(), calls=%async_computation.2 | async-start | bytes 9437184 | tf_op jit(solution)/shard_map/psum | solution.py:143
  400.0 7.4 copy-start.2
  400.0 3.9 copy-start.20
  405.1 4.3 slice-start.2
  409.4 3.6 copy-start.7
  418.7 398.6 %all-reduce.14.cloned.1.call-start = ((), (), s32[]{:S(2)}) async-start(), calls=%async_computation.3 | async-start | bytes 9437184 | tf_op jit(solution)/shard_map/psum | solution.py:192
  604.0 6.1 copy-start.10
  628.4 4.0 copy-start.6
  628.4 4.0 copy-start.8
  646.2 288.3 %all-reduce.16.cloned.1.call-start = ((), (), s32[]{:S(2)}) async-start(), calls=%async_computation.4 | async-start | bytes 14155776 | tf_op jit(solution)/shard_map/psum | solution.py:207
  646.3 6.7 copy-start.33
  646.3 13.1 %slice-start = ((s8[4718592]{0:T(1024)(128)(4,1)}), s8[4194304]{0:T(1024)(128)(4,1)S(1)}, s32[]{:S(2)}) async-start(s8[4718592]{0:T(1024)(128)(4,1)} %bitcast.65), calls=%async_computation.5 | async-start | bytes 8388608
  653.0 6.4 slice-start.1
  934.5 5.0 copy-start.13
  934.5 6.4 copy-start.12
  937.5 4.8 copy-start.1
  (19 other events, 28.4 us)
Sparse Core Ops, SparseCore 0:
  34.7 174.6 all-reduce.7
  224.2 170.9 all-reduce.9
  418.9 170.9 all-reduce.11
  646.4 170.9 all-reduce.13
  822.0 112.4 all-reduce.15
where the time goes:
time: 957 us; the launch traced here: 949 us
  waiting for transfers between devices  746 us (78%)
  matrix products  79.3 us (8%)
  other arithmetic  48.8 us (5%)
  local copies, waits for them, and re-layouts  32.5 us (3%)
  blocking collectives  26.2 us (3%)
  between operations  15.3 us (2%)
    psum x1, waiting for transfers between devices, body(): attn_total = lax.psum(partial_out, 'mp')  174 us
    psum x1, waiting for transfers between devices, body(): d_norm_one = d_res_two + lax.psum(up_part, 'mp')  171 us
    psum x1, waiting for transfers between devices, body(): down_total = lax.psum(partial_down, 'mp')  170 us
    psum x1, waiting for transfers between devices, body(): input_grad = d_res_one + lax.psum(token_part, 'mp')  121 us
    psum x1, waiting for transfers between devices, body(): lax.psum((grad_qkv, grad_qv_bias, grad_out, grad_out_bias, grad_gain_one,...  111 us
    psum x1, blocking collectives, body(): lax.psum((grad_qkv, grad_qv_bias, grad_out, grad_out_bias, grad_gain_one,...  26.2 us
  transfers between devices with their start and end apart: 5, of which 5 were waited for; matrix products, arithmetic and copies ran while one was open for 3% of the time, Pallas kernels for 0%

commit v1 on v0

v1 whole, which is shorter than its diff:
```python
import functools

import jax
import jax.numpy as jnp
from jax import lax
from jax.experimental import pallas as pl
from jax.experimental.pallas import tpu as pltpu
from jax.sharding import PartitionSpec as P

HEAD = 64
CORE = 1
norm_eps = 1e-12
highest = lax.Precision.HIGHEST
f32 = jnp.float32
bf16 = jnp.bfloat16


def dot(left, right, left_dim, right_dim):
    return lax.dot_general(
        left, right, (((left_dim,), (right_dim,)), ((), ())), preferred_element_type=f32
    )


def layer_norm(residual, gain_vec):
    row_mean = jnp.mean(residual, axis=-1, keepdims=True)
    centered = residual - row_mean
    inv_std = lax.rsqrt(jnp.mean(centered * centered, axis=-1, keepdims=True) + norm_eps)
    normed = centered * inv_std
    return (normed * gain_vec, normed, inv_std)


def norm_back(grad_rows, normed, inv_std, gain_vec):
    grad_normed = grad_rows * gain_vec
    grad_res = (
        grad_normed
        - jnp.mean(grad_normed, axis=-1, keepdims=True)
        - normed * jnp.mean(grad_normed * normed, axis=-1, keepdims=True)
    ) * inv_std
    return (grad_res, jnp.sum(grad_rows * normed, axis=0), jnp.sum(grad_rows, axis=0))


def gelu_exact(values_in):
    return 0.5 * values_in * (1.0 + lax.erf(values_in * 0.7071067811865476))


def gelu_slope(values_in):
    return (
        0.5 * (1.0 + lax.erf(values_in * 0.7071067811865476))
        + values_in * jnp.exp(-0.5 * values_in * values_in) * 0.3989422804014327
    )


def attend_kernel(qkv_ref, mask_ref, context_ref, probs_ref):
    query, key, value = qkv_ref[0, 0], qkv_ref[1, 0], qkv_ref[2, 0]
    scores = dot(key, query, 0, 0) + mask_ref[...]
    exponent = jnp.exp(scores - jnp.max(scores, axis=0, keepdims=True))
    total = jnp.sum(exponent, axis=0, keepdims=True)
    probs = (exponent / total).astype(bf16)
    probs_ref[0] = probs
    context_ref[0] = dot(value, probs, 1, 0).astype(bf16)


def attend(qkv, mask):
    heads, head, seq = qkv.shape[1:]
    return pl.pallas_call(
        attend_kernel,
        grid=(heads,),
        in_specs=[
            pl.BlockSpec((3, 1, head, seq), lambda h: (0, h, 0, 0)),
            pl.BlockSpec((seq, seq), lambda h: (0, 0)),
        ],
        out_specs=[
            pl.BlockSpec((1, head, seq), lambda h: (h, 0, 0)),
            pl.BlockSpec((1, seq, seq), lambda h: (h, 0, 0)),
        ],
        out_shape=[
            jax.ShapeDtypeStruct((heads, head, seq), bf16),
            jax.ShapeDtypeStruct((heads, seq, seq), bf16),
        ],
        compiler_params=pltpu.CompilerParams(vmem_limit_bytes=24 << 20),
        cost_estimate=pl.CostEstimate(
            flops=16 * heads * seq * seq * head,
            bytes_accessed=4 * heads * seq * seq,
            transcendentals=heads * seq * seq,
        ),
        name="attend",
    )(qkv, mask)


def attend_back_kernel(qkv_ref, probs_ref, context_ref, grad_ref, out_ref):
    query, key, value = qkv_ref[0, 0], qkv_ref[1, 0], qkv_ref[2, 0]
    probs = probs_ref[0]
    grad = grad_ref[0]
    shared = jnp.sum(grad.astype(f32) * context_ref[0].astype(f32), axis=0, keepdims=True)
    d_probs = dot(value, grad, 0, 0)
    d_scores = (probs.astype(f32) * (d_probs - shared)).astype(bf16)
    out_ref[0, 0] = (dot(key, d_scores, 1, 0) * HEAD**-0.5).astype(bf16)
    out_ref[1, 0] = dot(query, d_scores, 1, 1).astype(bf16)
    out_ref[2, 0] = dot(grad, probs, 1, 1).astype(bf16)


def attend_back(qkv, probs, context, grad):
    heads, head, seq = qkv.shape[1:]
    return pl.pallas_call(
        attend_back_kernel,
        grid=(heads,),
        in_specs=[
            pl.BlockSpec((3, 1, head, seq), lambda h: (0, h, 0, 0)),
            pl.BlockSpec((1, seq, seq), lambda h: (h, 0, 0)),
            pl.BlockSpec((1, head, seq), lambda h: (h, 0, 0)),
            pl.BlockSpec((1, head, seq), lambda h: (h, 0, 0)),
        ],
        out_specs=pl.BlockSpec((3, 1, head, seq), lambda h: (0, h, 0, 0)),
        out_shape=jax.ShapeDtypeStruct(qkv.shape, bf16),
        compiler_params=pltpu.CompilerParams(vmem_limit_bytes=24 << 20),
        cost_estimate=pl.CostEstimate(
            flops=32 * heads * seq * seq * head,
            bytes_accessed=2 * heads * seq * seq,
            transcendentals=0,
        ),
        name="attend_back",
    )(qkv, probs, context, grad)


def ordered_kernel(order, own_ref, got_ref, out_ref):
    rows = [ref[at, 0] for ref in (own_ref, got_ref) for at in order]
    out_ref[0] = jnp.concatenate(rows).astype(bf16)


def ordered(held):
    own, got, masks = held
    order = sorted(range(len(masks)), key=lambda at: masks[at])
    if own.shape[2] % 8:
        own, got = (jnp.concatenate([a[at] for at in order], axis=1)[None] for a in (own, got))
        order = [0]
    chips, group, strip, width = own.shape
    cuts = 2 if group == 1 else 1
    block = pl.BlockSpec((chips, 1, strip, width // cuts), lambda g, w: (0, g, 0, w))
    return pl.pallas_call(
        functools.partial(ordered_kernel, order),
        grid=(group, cuts),
        in_specs=[block, block],
        out_specs=pl.BlockSpec((1, 2 * chips * strip, width // cuts), lambda g, w: (g, 0, w)),
        out_shape=jax.ShapeDtypeStruct((group, 2 * chips * strip, width), bf16),
        compiler_params=pltpu.CompilerParams(vmem_limit_bytes=24 << 20),
        cost_estimate=pl.CostEstimate(flops=0, bytes_accessed=10 * own.size, transcendentals=0),
        name="ordered",
    )(own, got)


def natural_kernel(masks, me_ref, own_ref, got_ref, out_ref):
    strip = own_ref.shape[2]
    for core, ref in enumerate((own_ref, got_ref)):
        for at, mask in enumerate(masks):
            start = pl.multiple_of((me_ref[0] ^ (mask | core)) * strip, 8)
            out_ref[0, pl.ds(start, strip)] = ref[at, 0]


def natural(held, me):
    own, got, masks = held
    chips, group, strip, width = own.shape
    if strip % 8:
        stacked = jnp.concatenate([own, got])
        spots = [masks.index(m & ~CORE) + chips * (m & CORE) for m in range(2 * chips)]
        stacked = jnp.stack([stacked[at] for at in spots])
        return jnp.concatenate(
            [lax.dynamic_index_in_dim(stacked, me ^ j, 0, keepdims=False) for j in range(2 * chips)],
            axis=1,
        )
    cuts = 2 if group == 1 else 1
    block = pl.BlockSpec((chips, 1, strip, width // cuts), lambda g, w: (0, g, 0, w))
    return pl.pallas_call(
        functools.partial(natural_kernel, masks),
        grid=(group, cuts),
        in_specs=[pl.BlockSpec(memory_space=pltpu.SMEM), block, block],
        out_specs=pl.BlockSpec((1, 2 * chips * strip, width // cuts), lambda g, w: (g, 0, w)),
        out_shape=jax.ShapeDtypeStruct((group, 2 * chips * strip, width), f32),
        compiler_params=pltpu.CompilerParams(vmem_limit_bytes=24 << 20),
        cost_estimate=pl.CostEstimate(flops=0, bytes_accessed=16 * own.size, transcendentals=0),
        name="natural",
    )(me.astype(jnp.int32)[None], own, got)


def hold(array):
    return lax.optimization_barrier(array)


class Links:
    def __init__(self, dp_size, mp_size):
        self.dp_size, self.mp_size = dp_size, mp_size
        chip_bits = [1 << b for b in range(1, dp_size.bit_length() - 1)]
        self.orders = (chip_bits, chip_bits[::-1])
        self.chip_masks = list(range(0, dp_size, 2))

    def swap(self, array, bit):
        return hold(lax.ppermute(hold(array), "dp", [(i, i ^ bit) for i in range(self.dp_size)]))

    def ring(self, array):
        size = self.mp_size
        return hold(lax.ppermute(hold(array), "mp", [(i, (i + 1) % size) for i in range(size)]))

    def gather(self, pieces):
        stacks = [piece[None] for piece in pieces]
        masks = [[0], [0]]
        for step in range(len(self.orders[0])):
            got = [self.swap(stack, self.orders[side][step]) for side, stack in enumerate(stacks)]
            for side in range(2):
                bit = self.orders[side][step]
                stacks[side] = jnp.concatenate([stacks[side], got[side]])
                masks[side] = masks[side] + [m ^ bit for m in masks[side]]
        return [(stack, self.swap(stack, CORE), order) for stack, order in zip(stacks, masks)]

    def scatter(self, parts, side):
        for bit in reversed(self.orders[side]):
            kept = [m for m in parts if not m & bit]
            got = self.swap(jnp.stack([parts[m | bit] for m in kept]), bit)
            parts = {m: parts[m] + got[at] for at, m in enumerate(kept)}
        return parts[0]


def body(
    tokens,
    segment_ids,
    lengths,
    cotangent,
    w_qkv,
    b_qv,
    w_out,
    b_out,
    gain_one,
    shift_one,
    w_up,
    b_up,
    w_down,
    b_down,
    gain_two,
    w_head,
    b_head,
    *,
    dp_size,
    mp_size,
):
    links = Links(dp_size, mp_size)
    row_count, seq = segment_ids.shape
    width = tokens.shape[1]
    local_width = w_qkv.shape[2]
    heads = local_width // HEAD
    hidden = w_up.shape[1]
    groups = 4 * heads
    half_groups = groups // 2
    strip = HEAD // dp_size
    span = hidden // dp_size
    me = lax.axis_index("dp")
    z = lax.axis_index("mp")
    masks = links.chip_masks + [m | CORE for m in links.chip_masks]
    half = dp_size // 2
    later = list(range(1, mp_size)) + [0]

    owners = [i for i in range(mp_size) if i != mp_size // 2][:row_count]
    row_of = [owners.index(i) if i in owners else 0 for i in range(mp_size)]
    row = jnp.asarray(row_of, jnp.int32)[z]
    active = jnp.asarray([float(i in owners) for i in range(mp_size)], f32)[z]

    attn_own = jnp.concatenate(
        [jnp.transpose(w_qkv, (1, 2, 0)).reshape(3 * heads, HEAD, width), w_out.reshape(heads, HEAD, width)]
    ).reshape(groups, dp_size, strip, width)
    up_own = w_up.T.reshape(dp_size, span, width)
    down_own = w_down.reshape(dp_size, span, width)

    def slice_of(array, at, axis):
        return lax.dynamic_index_in_dim(array, at, axis, keepdims=False)

    attn_mine = slice_of(attn_own, me, 1).astype(f32)
    ffn_mine = tuple(slice_of(own, me, 0).astype(f32)[None] for own in (up_own, down_own))
    pieces = {"attn": (attn_mine[:half_groups], attn_mine[half_groups:]), "ffn": ffn_mine}

    def own_order(array, axis):
        return jnp.concatenate(
            [lax.dynamic_slice_in_dim(array, me ^ m, 1, axis) for m in masks], axis=axis
        )

    attn_w = [own_order(attn_own, 1).reshape(groups, HEAD, width)]
    ffn_w = [
        [
            own_order(up_own, 0).reshape(hidden, width),
            own_order(down_own, 0).reshape(hidden, width),
        ]
    ]
    going = pieces["attn"]
    for k in range(1, mp_size):
        going = tuple(links.ring(piece) for piece in going)
        attn_w.append(jnp.concatenate([ordered(held) for held in links.gather(going)]))
    going = pieces["ffn"]
    for k in range(1, mp_size):
        going = tuple(links.ring(piece) for piece in going)
        ffn_w.append([ordered(held).reshape(hidden, width) for held in links.gather(going)])

    small = jnp.concatenate([b_qv.astype(f32).reshape(-1), b_up.astype(f32)])
    small = lax.all_gather(small, "mp")
    slice_pick = (
        jnp.asarray(masks, jnp.int32)[:, None] ^ me
    ) == jnp.arange(dp_size, dtype=jnp.int32)[None, :]
    shard_pick = (
        (z - jnp.arange(mp_size, dtype=jnp.int32)) % mp_size
    )[:, None] == jnp.arange(mp_size, dtype=jnp.int32)[None, :]

    def pick(flags, array, axis):
        moved = jnp.expand_dims(array, axis)
        shape = [1] * moved.ndim
        shape[axis], shape[axis + 1] = flags.shape
        return jnp.sum(jnp.where(flags.reshape(shape), moved, 0.0), axis=axis + 1)

    small = pick(shard_pick, small, 0)
    qv_bias = small[:, : 2 * local_width].reshape(mp_size, 2, heads, dp_size, strip)
    qv_bias = pick(slice_pick, qv_bias, 3).reshape(mp_size, 2, heads * HEAD)
    up_bias = pick(slice_pick, small[:, 2 * local_width :].reshape(mp_size, dp_size, span), 1)
    up_bias = up_bias.reshape(mp_size, hidden)

    b_out_f = b_out.astype(f32)
    gain_one_f = gain_one.astype(f32)
    shift_one_f = shift_one.astype(f32)
    b_down_f = b_down.astype(f32)
    gain_two_f = gain_two.astype(f32)
    w_head_f = w_head.astype(f32)
    b_head_f = b_head.astype(f32)

    own_tokens = lax.dynamic_slice_in_dim(tokens, row * seq, seq, 0)
    own_segments = slice_of(segment_ids, row, 0)
    own_length = slice_of(lengths, row, 0)
    own_cotangent = lax.dynamic_slice_in_dim(cotangent, row * seq, seq, 0) * active
    positions = jnp.arange(seq)
    valid = (positions < own_length).astype(f32)
    allowed = (own_segments[:, None] == own_segments[None, :]) & (
        (positions[:, None] < own_length) | (positions[:, None] == positions[None, :])
    )
    mask = jnp.where(allowed, 0.0, -1e30).astype(f32)

    part = heads * HEAD
    scale_col = jnp.concatenate([jnp.full((part,), HEAD**-0.5, f32), jnp.ones((2 * part,), f32)])
    qkv, context, probs = [], [], []
    branch = own_tokens.astype(f32) + b_out_f
    for k in range(mp_size):
        bias_col = jnp.concatenate([qv_bias[k, 0], jnp.zeros((part,), f32), qv_bias[k, 1]])
        w_k = attn_w[k][: 3 * heads].reshape(3 * part, width)
        made = (dot(w_k, own_tokens, 1, 1) + bias_col[:, None]) * scale_col[:, None]
        qkv.append(made.astype(bf16).reshape(3, heads, HEAD, seq))
        context_k, probs_k = attend(qkv[k], mask)
        context.append(context_k.reshape(part, seq))
        probs.append(probs_k)
        branch = branch + dot(context[k], attn_w[k][3 * heads :].reshape(part, width), 0, 0)
    scaled_one, normed_one, inv_one = layer_norm(branch, gain_one_f)
    norm_one = scaled_one + shift_one_f
    norm_one_low = norm_one.astype(bf16)
    pre, act = [], []
    res_two = norm_one + b_down_f
    for k in range(mp_size):
        pre.append(dot(norm_one_low, ffn_w[k][0], 1, 1) + up_bias[k])
        act.append(gelu_exact(pre[k]).astype(bf16))
        res_two = res_two + dot(act[k], ffn_w[k][1], 1, 0)
    norm_two, normed_two, inv_two = layer_norm(res_two, gain_two_f)
    logits = jnp.sum(norm_two * w_head_f, axis=-1) + b_head_f[0]
    own_weight = jax.nn.softplus(logits) * valid
    all_weights = lax.all_gather(own_weight, "mp")
    token_weight = jnp.concatenate([all_weights[i] for i in owners])

    d_logits = own_cotangent * valid * jax.nn.sigmoid(logits)
    grad_head = jnp.sum(d_logits[:, None] * norm_two, axis=0)
    grad_head_bias = jnp.sum(d_logits)[None]
    d_res_two, grad_gain_two, _ = norm_back(
        d_logits[:, None] * w_head_f, normed_two, inv_two, gain_two_f
    )
    grad_down_bias = jnp.sum(d_res_two, axis=0)
    d_res_two_low = d_res_two.astype(bf16)

    cut = hidden // 2
    d_norm_one = d_res_two
    grad_up_bias = [None] * mp_size
    ffn_going = None
    for k in later:
        d_hidden = dot(d_res_two_low, ffn_w[k][1], 1, 1) * gelu_slope(pre[k])
        grad_up_bias[k] = jnp.sum(d_hidden, axis=0)
        d_hidden_low = d_hidden.astype(bf16)
        sums = []
        for side, (left, right) in enumerate(((d_hidden_low, norm_one_low), (act[k], d_res_two_low))):
            got = links.swap(dot(left[:, cut:], right, 0, 0), CORE)
            kept = (dot(left[:, :cut], right, 0, 0) + got).reshape(half, span, width)
            parts = {m: kept[at] for at, m in enumerate(links.chip_masks)}
            sums.append(links.scatter(parts, side))
        if ffn_going is not None:
            sums = [one + two for one, two in zip(sums, ffn_going)]
        ffn_going = tuple(links.ring(one) for one in sums) if k else tuple(sums)
        d_norm_one = d_norm_one + dot(d_hidden_low, ffn_w[k][0], 1, 0)

    d_res_one, grad_gain_one, grad_shift_one = norm_back(
        d_norm_one, normed_one, inv_one, gain_one_f
    )
    grad_out_bias = jnp.sum(d_res_one, axis=0)
    d_res_one_low = d_res_one.astype(bf16)
    input_row = d_res_one
    grad_qv = [None] * mp_size
    attn_going = None
    for k in later:
        w_out_k = attn_w[k][3 * heads :].reshape(part, width)
        d_context = dot(w_out_k, d_res_one_low, 1, 1).astype(bf16).reshape(heads, HEAD, seq)
        d_qkv = attend_back(qkv[k], probs[k], context[k].reshape(heads, HEAD, seq), d_context)
        d_qkv_rows = d_qkv.reshape(3 * part, seq)
        grad_qv[k] = jnp.stack(
            [jnp.sum(d_qkv_rows[:part].astype(f32), axis=1), jnp.sum(d_qkv_rows[2 * part :].astype(f32), axis=1)]
        )
        input_row = input_row + dot(
            d_qkv_rows, attn_w[k][: 3 * heads].reshape(3 * part, width), 0, 0
        )
        grad_k = jnp.concatenate(
            [dot(d_qkv_rows, own_tokens, 1, 0), dot(context[k], d_res_one_low, 1, 0)]
        ).reshape(groups, 2, half, strip, width)
        sums = []
        for side in range(2):
            mine = grad_k[side * half_groups : (side + 1) * half_groups]
            got = links.swap(mine[:, 1], CORE)
            kept = mine[:, 0] + got
            parts = {m: kept[:, at] for at, m in enumerate(links.chip_masks)}
            sums.append(links.scatter(parts, side))
        if attn_going is not None:
            sums = [one + two for one, two in zip(sums, attn_going)]
        attn_going = tuple(links.ring(one) for one in sums) if k else tuple(sums)

    rows = {0: input_row}
    for k in range(1, mp_size):
        rows[k] = links.ring(rows[k - 1])
    input_grad = jnp.concatenate(
        [
            functools.reduce(
                lambda other, k: jnp.where((z - k) % mp_size == owner, rows[k], other),
                range(1, mp_size),
                rows[0],
            )
            for owner in owners
        ]
    )

    ffn_held = links.gather([one[None] for one in ffn_going])
    grad_up = natural(ffn_held[0], me).reshape(hidden, width).T
    grad_down = natural(ffn_held[1], me).reshape(hidden, width)
    attn_grad = jnp.concatenate([natural(held, me) for held in links.gather(attn_going)])
    grad_qkv = jnp.transpose(
        attn_grad[: 3 * heads].reshape(3, local_width, width), (2, 0, 1)
    )
    grad_out = attn_grad[3 * heads :].reshape(local_width, width)

    up_b = jnp.stack(grad_up_bias).reshape(mp_size, dp_size, span)
    up_b = pick(slice_pick.T, pick(shard_pick.T, up_b, 0), 1).reshape(-1)
    qv_b = jnp.stack(grad_qv).reshape(mp_size, 2, heads, dp_size, strip)
    qv_b = pick(slice_pick.T, pick(shard_pick.T, qv_b, 0), 3).reshape(-1)
    early = [up_b, grad_out_bias, grad_gain_one, grad_shift_one, grad_down_bias, grad_gain_two, grad_head, grad_head_bias]
    early_sum = lax.psum(jnp.concatenate(early), ("dp", "mp"))
    late_sum = lax.psum(qv_b, ("dp", "mp")).reshape(mp_size, 2, local_width)
    grad_qv_bias = slice_of(late_sum, z, 0)
    early_parts, at = [], 0
    for one in early:
        early_parts.append(early_sum[at : at + one.shape[0]])
        at += one.shape[0]
    grad_up_bias_out = slice_of(early_parts[0].reshape(mp_size, hidden), z, 0)
    (
        grad_out_bias,
        grad_gain_one,
        grad_shift_one,
        grad_down_bias,
        grad_gain_two,
        grad_head,
        grad_head_bias,
    ) = early_parts[1:]
    return (
        token_weight,
        input_grad,
        grad_qkv,
        grad_qv_bias,
        grad_out,
        grad_out_bias,
        grad_gain_one,
        grad_shift_one,
        grad_up,
        grad_up_bias_out,
        grad_down,
        grad_down_bias,
        grad_gain_two,
        grad_head,
        grad_head_bias,
    )


def solution(mesh):
    placed = (
        P("dp", None),
        P("dp", None),
        P("dp"),
        P("dp"),
        P(None, None, "mp"),
        P(None, "mp"),
        P("mp", None),
        P(),
        P(),
        P(),
        P(None, "mp"),
        P("mp"),
        P("mp", None),
        P(),
        P(),
        P(),
        P(),
    )
    return jax.shard_map(
        functools.partial(body, dp_size=mesh.shape["dp"], mp_size=mesh.shape["mp"]),
        mesh=mesh,
        in_specs=placed,
        out_specs=(
            P("dp"),
            P("dp", None),
            P(None, None, "mp"),
            P(None, "mp"),
            P("mp", None),
            P(),
            P(),
            P(),
            P(None, "mp"),
            P("mp"),
            P("mp", None),
            P(),
            P(),
            P(),
            P(),
        ),
        check_vma=False,
    )
```

time: 957 us -> 644 us (0.67)
  waiting for transfers between devices: 746 us -> 279 us
  starting transfers between devices: 0.79 us -> 93.9 us
  blocking collectives: 26.2 us -> 88.2 us
  Pallas kernels: 0 us -> 34.7 us
  other arithmetic: 48.8 us -> 28.6 us
  matrix products: 79.3 us -> 63.8 us
    psum x5 -> x0, waiting for transfers between devices: 746 us -> none  [the longest x1 174 us: body(): attn_total = lax.psum(partial_out, 'mp')]
    ppermute x0 -> x123, waiting for transfers between devices: none -> 279 us  [the longest x27 146 us: ring(): lax.ppermute(hold(array), 'mp', [(i, (i + 1) % size) for i in range(size)])]
    ppermute x0 -> x123, starting transfers between devices: none -> 93.9 us  [the longest x96 78.3 us: swap(): lax.ppermute(hold(array), 'dp', [(i, i ^ bit) for i in range(self.dp_size)])]
    all_gather x0 -> x2, blocking collectives: none -> 50.3 us  [the longest x1 33.7 us: body(): all_weights = lax.all_gather(own_weight, 'mp')]
    pallas_call x0 -> x24, Pallas kernels: none -> 34.7 us  [the longest x4 10.3 us: attend_back(): pl.pallas_call(attend_back_kernel, grid=(heads,), in_specs=[pl.BlockSpec(...]
    reduce_sum x7 -> x13, other arithmetic: 18.9 us -> 3.1 us  [the longest x7 1.16 us: pick(): return jnp.sum(jnp.where(flags.reshape(shape), moved, 0.0), axis=axis + 1)]
    convert_element_type x11 -> x10, other arithmetic: 13.6 us -> 1.53 us  [the longest x1 1.04 us: body(): attn_mine = slice_of(attn_own, me, 1).astype(f32)]
    dot_general x19 -> x56, matrix products: 75.8 us -> 63.8 us  [dot(): lax.dot_general(left, right, (((left_dim,), (right_dim,)), ((), ())), pre...]
  transfers between devices with their start and end apart: 5 -> 123, of which waited for: 5 -> 51; matrix products, arithmetic and copies ran while one was open for 3% -> 9% of each run, Pallas kernels for 0% -> 3%
where the time goes in v1:
time: 644 us; the launch traced here: 637 us
  waiting for transfers between devices  279 us (43%)
  starting transfers between devices  93.9 us (15%)
  blocking collectives  88.2 us (14%)
  matrix products  63.8 us (10%)
  local copies, waits for them, and re-layouts  41.5 us (6%)
  Pallas kernels  34.7 us (5%)
  other arithmetic  28.6 us (4%)
  between operations  7.15 us (1%)
    ppermute x27, waiting for transfers between devices, ring(): lax.ppermute(hold(array), 'mp', [(i, (i + 1) % size) for i in range(size)])  146 us
    ppermute x96, waiting for transfers between devices, swap(): lax.ppermute(hold(array), 'dp', [(i, i ^ bit) for i in range(self.dp_size)])  132 us
    ppermute x96, starting transfers between devices, swap(): lax.ppermute(hold(array), 'dp', [(i, i ^ bit) for i in range(self.dp_size)])  78.3 us
    dot_general x56, matrix products, dot(): lax.dot_general(left, right, (((left_dim,), (right_dim,)), ((), ())), pre...  63.8 us
    psum x1, blocking collectives, body(): late_sum = lax.psum(qv_b, ('dp', 'mp')).reshape(mp_size, 2, local_width)  37.9 us
    all_gather x1, blocking collectives, body(): all_weights = lax.all_gather(own_weight, 'mp')  33.7 us
    unnamed x164, local copies, waits for them, and re-layouts  25.1 us
    all_gather x1, blocking collectives, body(): small = lax.all_gather(small, 'mp')  16.7 us
  transfers between devices with their start and end apart: 123, of which 51 were waited for; matrix products, arithmetic and copies ran while one was open for 9% of the time, Pallas kernels for 3%

profile of v1, /device:TPU:0, one launch (start us, length us, event | category | flops | bytes accessed | tf_op | source)
XLA Modules:
  0.0 636.8 jit_solution(11969731564413789667)
XLA Ops:
  22.9 16.7 %all-gather.1 = f32[4,1,1152]{2,1,0:T(1,128)S(1)} all-gather(f32[1,1,1152]{2,1,0:T(1,128)S(1)} %reshape.646), channel_id=2, replica_groups=mesh['dp'=8,'mp'=4] {'mp'}, dimensions={0}, use_global_device_ids=true | all-gather | bytes 23040 | tf_op jit(solution)/shard_map/all_gather | solution.py:299
  55.0 4.7 collective-permute-done.8
  95.7 5.7 collective-permute-done.40
  113.3 10.2 %collective-permute-done.41 = f32[1,1,96,768]{3,2,1,0:T(8,128)S(1)} collective-permute-done((f32[1,1,96,768]{3,2,1,0:T(8,128)S(1)}, f32[1,1,96,768]{3,2,1,0:T(8,128)S(1)}, u32[]{:S(2)}, u32[]{:S(2)}) %collective-permute-start.41) | collective-permute-done | bytes 294944 | tf_op jit(solution)/shard_map/ppermute | solution.py:196
  235.8 37.9 %all-reduce = (f32[4,2,192]{2,1,0:T(2,128)}, f32[7681]{0:T(1024)S(1)}) all-reduce(f32[4,2,192]{2,1,0:T(2,128)S(1)} %reshape.636, f32[7681]{0:T(1024)S(1)} %constant_dynamic-update-slice_fusion.1), channel_id=1, replica_groups=mesh['dp'=8,'mp'=4] {'dp','mp'}, use_global_device_ids=true, to_apply=%region_22.23 | all-reduce | flops 9217 | bytes 73736 | tf_op jit(solution)/shard_map/psum | solution.py:456
  330.6 4.9 collective-permute-done.74
  336.1 4.8 collective-permute-done.56
  343.5 4.3 collective-permute-done.81
  348.7 6.1 collective-permute-done.63
  363.9 35.8 %collective-permute-done.82 = f32[6,8,768]{2,1,0:T(8,128)S(1)} collective-permute-done((f32[6,8,768]{2,1,0:T(8,128)S(1)}, f32[6,8,768]{2,1,0:T(8,128)S(1)}, u32[]{:S(2)}, u32[]{:S(2)}) %collective-permute-start.82) | collective-permute-done | bytes 147488 | tf_op jit(solution)/shard_map/ppermute | solution.py:200
  402.1 6.9 %collective-permute-done.83 = f32[6,8,768]{2,1,0:T(8,128)S(1)} collective-permute-done((f32[6,8,768]{2,1,0:T(8,128)S(1)}, f32[6,8,768]{2,1,0:T(8,128)S(1)}, u32[]{:S(2)}, u32[]{:S(2)}) %collective-permute-start.83) | collective-permute-done | bytes 147488 | tf_op jit(solution)/shard_map/ppermute | solution.py:200
  409.1 6.9 %collective-permute-done.65 = f32[6,8,768]{2,1,0:T(8,128)S(1)} collective-permute-done((f32[6,8,768]{2,1,0:T(8,128)S(1)}, f32[6,8,768]{2,1,0:T(8,128)S(1)}, u32[]{:S(2)}, u32[]{:S(2)}) %collective-permute-start.65) | collective-permute-done | bytes 147488 | tf_op jit(solution)/shard_map/ppermute | solution.py:200
  418.4 4.3 collective-permute-done.84
  430.2 8.8 %collective-permute-done.97 = f32[2,96,768]{2,1,0:T(8,128)S(1)} collective-permute-done((f32[2,96,768]{2,1,0:T(8,128)S(1)}, f32[2,96,768]{2,1,0:T(8,128)S(1)}, u32[]{:S(2)}, u32[]{:S(2)}) %collective-permute-start.97) | collective-permute-done | bytes 589856 | tf_op jit(solution)/shard_map/ppermute | solution.py:196
  440.3 11.3 %collective-permute-done.94 = f32[2,96,768]{2,1,0:T(8,128)S(1)} collective-permute-done((f32[2,96,768]{2,1,0:T(8,128)S(1)}, f32[2,96,768]{2,1,0:T(8,128)S(1)}, u32[]{:S(2)}, u32[]{:S(2)}) %collective-permute-start.94) | collective-permute-done | bytes 589856 | tf_op jit(solution)/shard_map/ppermute | solution.py:196
  452.1 12.1 %collective-permute-done.91 = f32[2,96,768]{2,1,0:T(8,128)S(1)} collective-permute-done((f32[2,96,768]{2,1,0:T(8,128)S(1)}, f32[2,96,768]{2,1,0:T(8,128)S(1)}, u32[]{:S(2)}, u32[]{:S(2)}) %collective-permute-start.91) | collective-permute-done | bytes 589856 | tf_op jit(solution)/shard_map/ppermute | solution.py:196
  464.7 21.5 %collective-permute-done.116 = f32[1,96,768]{2,1,0:T(8,128)S(1)} collective-permute-done((f32[1,96,768]{2,1,0:T(8,128)S(1)}, f32[1,96,768]{2,1,0:T(8,128)S(1)}, u32[]{:S(2)}, u32[]{:S(2)}) %collective-permute-start.116) | collective-permute-done | bytes 294944 | tf_op jit(solution)/shard_map/ppermute | solution.py:196
  489.0 9.1 %collective-permute-done.117 = f32[96,768]{1,0:T(8,128)S(1)} collective-permute-done((f32[96,768]{1,0:T(8,128)S(1)}, f32[96,768]{1,0:T(8,128)S(1)}, u32[]{:S(2)}, u32[]{:S(2)}) %collective-permute-start.117) | collective-permute-done | bytes 294944 | tf_op jit(solution)/shard_map/ppermute | solution.py:200
  498.2 6.2 collective-permute-done.99
  507.0 37.5 %collective-permute-done.118 = f32[96,768]{1,0:T(8,128)S(1)} collective-permute-done((f32[96,768]{1,0:T(8,128)S(1)}, f32[96,768]{1,0:T(8,128)S(1)}, u32[]{:S(2)}, u32[]{:S(2)}) %collective-permute-start.118) | collective-permute-done | bytes 294944 | tf_op jit(solution)/shard_map/ppermute | solution.py:200
  544.6 4.5 collective-permute-done.100
  554.6 6.4 %collective-permute-done.101 = f32[96,768]{1,0:T(8,128)S(1)} collective-permute-done((f32[96,768]{1,0:T(8,128)S(1)}, f32[96,768]{1,0:T(8,128)S(1)}, u32[]{:S(2)}, u32[]{:S(2)}) %collective-permute-start.101) | collective-permute-done | bytes 294944 | tf_op jit(solution)/shard_map/ppermute | solution.py:200
  562.3 33.7 %all-gather.2 = f32[4,1,512]{2,1,0:T(1,128)S(1)} all-gather(f32[1,1,512]{2,1,0:T(1,128)S(1)} %fusion.182), channel_id=1, replica_groups=mesh['dp'=8,'mp'=4] {'mp'}, dimensions={0}, use_global_device_ids=true | all-gather | bytes 10240 | tf_op jit(solution)/shard_map/all_gather | solution.py:363
  602.9 4.5 collective-permute-done.121
  (708 shorter events, 325.0 us)
Async XLA Ops:
  2.4 41.6 %collective-permute-start.4 = (f32[6,8,768]{2,1,0:T(8,128)}, f32[6,8,768]{2,1,0:T(8,128)}, u32[]{:S(2)}, u32[]{:S(2)}) collective-permute-start(f32[6,8,768]{2,1,0:T(8,128)} %get-tuple-element.188), channel_id=1, source_target_pairs={{0,1},{1,2},{2,3},{3,0},{4,5},{5,6},{6,7},{7,4},{8,9},{9,10},{10,1... | collective-permute-start | bytes 442376 | tf_op jit(solution)/shard_map/ppermute | solution.py:200
  5.5 46.5 %collective-permute-start = (f32[6,8,768]{2,1,0:T(8,128)}, f32[6,8,768]{2,1,0:T(8,128)}, u32[]{:S(2)}, u32[]{:S(2)}) collective-permute-start(f32[6,8,768]{2,1,0:T(8,128)} %get-tuple-element.187), channel_id=1, source_target_pairs={{0,1},{1,2},{2,3},{3,0},{4,5},{5,6},{6,7},{7,4},{8,9},{9,10},{10,1... | collective-permute-start | bytes 442376 | tf_op jit(solution)/shard_map/ppermute | solution.py:200
  15.8 45.8 %collective-permute-start.28 = (f32[1,96,768]{2,1,0:T(8,128)}, f32[1,96,768]{2,1,0:T(8,128)S(1)}, u32[]{:S(2)}, u32[]{:S(2)}) collective-permute-start(f32[1,96,768]{2,1,0:T(8,128)} %get-tuple-element.168), channel_id=1, source_target_pairs={{0,1},{1,2},{2,3},{3,0},{4,5},{5,6},{6,7},{7,4},{8,9},{9,10},{10,1... | collective-permute-start | bytes 884744 | tf_op jit(solution)/shard_map/ppermute | solution.py:200
  17.4 46.6 %collective-permute-start.24 = (f32[1,96,768]{2,1,0:T(8,128)}, f32[1,96,768]{2,1,0:T(8,128)S(1)}, u32[]{:S(2)}, u32[]{:S(2)}) collective-permute-start(f32[1,96,768]{2,1,0:T(8,128)} %get-tuple-element.235), channel_id=1, source_target_pairs={{0,1},{1,2},{2,3},{3,0},{4,5},{5,6},{6,7},{7,4},{8,9},{9,10},{10,1... | collective-permute-start | bytes 884744 | tf_op jit(solution)/shard_map/ppermute | solution.py:200
  357.5 59.9 %collective-permute-start.48 = (f32[512,768]{1,0:T(8,128)S(1)}, f32[512,768]{1,0:T(8,128)S(1)}, u32[]{:S(2)}, u32[]{:S(2)}) collective-permute-start(f32[512,768]{1,0:T(8,128)S(1)} %add_add_fusion), channel_id=1, source_target_pairs={{0,1},{1,2},{2,3},{3,0},{4,5},{5,6},{6,7},{7,4},{8,9},{9,10},{10,1... | collective-permute-start | bytes 4718600 | tf_op jit(solution)/shard_map/ppermute | solution.py:200
  358.6 41.1 %collective-permute-start.82 = (f32[6,8,768]{2,1,0:T(8,128)S(1)}, f32[6,8,768]{2,1,0:T(8,128)S(1)}, u32[]{:S(2)}, u32[]{:S(2)}) collective-permute-start(f32[6,8,768]{2,1,0:T(8,128)S(1)} %fusion.137), channel_id=1, source_target_pairs={{0,1},{1,2},{2,3},{3,0},{4,5},{5,6},{6,7},{7,4},{8,9},{9,10},{10,1... | collective-permute-start | bytes 442376 | tf_op jit(solution)/shard_map/ppermute | solution.py:200
  360.0 42.1 %collective-permute-start.64 = (f32[6,8,768]{2,1,0:T(8,128)S(1)}, f32[6,8,768]{2,1,0:T(8,128)S(1)}, u32[]{:S(2)}, u32[]{:S(2)}) collective-permute-start(f32[6,8,768]{2,1,0:T(8,128)S(1)} %fusion.149), channel_id=1, source_target_pairs={{0,1},{1,2},{2,3},{3,0},{4,5},{5,6},{6,7},{7,4},{8,9},{9,10},{10,1... | collective-permute-start | bytes 442376 | tf_op jit(solution)/shard_map/ppermute | solution.py:200
  361.0 62.9 %collective-permute-start.106 = (f32[2,96,768]{2,1,0:T(8,128)S(1)}, f32[2,96,768]{2,1,0:T(8,128)S(1)}, u32[]{:S(2)}, u32[]{:S(2)}) collective-permute-start(f32[2,96,768]{2,1,0:T(8,128)S(1)} %pad_maximum_fusion.36), channel_id=1, source_target_pairs={{0,8},{4,12},{8,0},{12,4},{16,24},{20,28},{24,16},{28,20},{1,9},{5... | collective-permute-start | bytes 1769480 | tf_op jit(solution)/shard_map/ppermute | solution.py:196
  362.7 62.0 %collective-permute-start.109 = (f32[2,96,768]{2,1,0:T(8,128)S(1)}, f32[2,96,768]{2,1,0:T(8,128)S(1)}, u32[]{:S(2)}, u32[]{:S(2)}) collective-permute-start(f32[2,96,768]{2,1,0:T(8,128)S(1)} %pad_maximum_fusion.37), channel_id=1, source_target_pairs={{0,8},{4,12},{8,0},{12,4},{16,24},{20,28},{24,16},{28,20},{1,9},{5... | collective-permute-start | bytes 1769480 | tf_op jit(solution)/shard_map/ppermute | solution.py:196
  424.7 39.5 %collective-permute-start.91 = (f32[2,96,768]{2,1,0:T(8,128)S(1)}, f32[2,96,768]{2,1,0:T(8,128)S(1)}, u32[]{:S(2)}, u32[]{:S(2)}) collective-permute-start(f32[2,96,768]{2,1,0:T(8,128)S(1)} %pad_maximum_fusion.32), channel_id=1, source_target_pairs={{0,16},{4,20},{8,24},{12,28},{16,0},{20,4},{24,8},{28,12},{1,17},{... | collective-permute-start | bytes 1769480 | tf_op jit(solution)/shard_map/ppermute | solution.py:196
  426.2 60.4 %collective-permute-start.88 = (f32[2,96,768]{2,1,0:T(8,128)S(1)}, f32[2,96,768]{2,1,0:T(8,128)S(1)}, u32[]{:S(2)}, u32[]{:S(2)}) collective-permute-start(f32[2,96,768]{2,1,0:T(8,128)S(1)} %pad_maximum_fusion.31), channel_id=1, source_target_pairs={{0,16},{4,20},{8,24},{12,28},{16,0},{20,4},{24,8},{28,12},{1,17},{... | collective-permute-start | bytes 1769480 | tf_op jit(solution)/shard_map/ppermute | solution.py:196
  429.4 57.2 %collective-permute-start.113 = (f32[1,96,768]{2,1,0:T(8,128)S(1)}, f32[1,96,768]{2,1,0:T(8,128)S(1)}, u32[]{:S(2)}, u32[]{:S(2)}) collective-permute-start(f32[1,96,768]{2,1,0:T(8,128)S(1)} %slice_add_fusion.1), channel_id=1, source_target_pairs={{0,16},{4,20},{8,24},{12,28},{16,0},{20,4},{24,8},{28,12},{1,17},{... | collective-permute-start | bytes 884744 | tf_op jit(solution)/shard_map/ppermute | solution.py:196
  438.9 47.3 %collective-permute-start.116 = (f32[1,96,768]{2,1,0:T(8,128)S(1)}, f32[1,96,768]{2,1,0:T(8,128)S(1)}, u32[]{:S(2)}, u32[]{:S(2)}) collective-permute-start(f32[1,96,768]{2,1,0:T(8,128)S(1)} %slice_add_fusion), channel_id=1, source_target_pairs={{0,16},{4,20},{8,24},{12,28},{16,0},{20,4},{24,8},{28,12},{1,17},{... | collective-permute-start | bytes 884744 | tf_op jit(solution)/shard_map/ppermute | solution.py:196
  451.6 34.8 %collective-permute-start.98 = (f32[1,96,768]{2,1,0:T(8,128)S(1)}, f32[1,96,768]{2,1,0:T(8,128)S(1)}, u32[]{:S(2)}, u32[]{:S(2)}) collective-permute-start(f32[1,96,768]{2,1,0:T(8,128)S(1)} %slice_add_fusion.4), channel_id=1, source_target_pairs={{0,8},{4,12},{8,0},{12,4},{16,24},{20,28},{24,16},{28,20},{1,9},{5... | collective-permute-start | bytes 884744 | tf_op jit(solution)/shard_map/ppermute | solution.py:196
  486.6 75.0 %collective-permute-start.49 = (f32[512,768]{1,0:T(8,128)S(1)}, f32[512,768]{1,0:T(8,128)}, u32[]{:S(2)}, u32[]{:S(2)}) collective-permute-start(f32[512,768]{1,0:T(8,128)S(1)} %collective-permute-done.48), channel_id=1, source_target_pairs={{0,1},{1,2},{2,3},{3,0},{4,5},{5,6},{6,7},{7,4},{8,9},{9,10},{10,1... | collective-permute-start | bytes 4718600 | tf_op jit(solution)/shard_map/ppermute | solution.py:200
  498.2 46.3 %collective-permute-start.118 = (f32[96,768]{1,0:T(8,128)S(1)}, f32[96,768]{1,0:T(8,128)S(1)}, u32[]{:S(2)}, u32[]{:S(2)}) collective-permute-start(f32[96,768]{1,0:T(8,128)S(1)} %fusion.105), channel_id=1, source_target_pairs={{0,1},{1,2},{2,3},{3,0},{4,5},{5,6},{6,7},{7,4},{8,9},{9,10},{10,1... | collective-permute-start | bytes 884744 | tf_op jit(solution)/shard_map/ppermute | solution.py:200
  504.5 44.6 %collective-permute-start.100 = (f32[96,768]{1,0:T(8,128)S(1)}, f32[96,768]{1,0:T(8,128)S(1)}, u32[]{:S(2)}, u32[]{:S(2)}) collective-permute-start(f32[96,768]{1,0:T(8,128)S(1)} %fusion.117), channel_id=1, source_target_pairs={{0,1},{1,2},{2,3},{3,0},{4,5},{5,6},{6,7},{7,4},{8,9},{9,10},{10,1... | collective-permute-start | bytes 884744 | tf_op jit(solution)/shard_map/ppermute | solution.py:200
  504.6 44.7 %collective-permute-start.107 = (f32[1,96,768]{2,1,0:T(8,128)S(1)}, f32[1,96,768]{2,1,0:T(8,128)S(1)}, u32[]{:S(2)}, u32[]{:S(2)}) collective-permute-start(f32[1,96,768]{2,1,0:T(8,128)S(1)} %slice_add_fusion.3), channel_id=1, source_target_pairs={{0,16},{4,20},{8,24},{12,28},{16,0},{20,4},{24,8},{28,12},{1,17},{... | collective-permute-start | bytes 884744 | tf_op jit(solution)/shard_map/ppermute | solution.py:196
  506.0 43.9 %collective-permute-start.89 = (f32[1,96,768]{2,1,0:T(8,128)S(1)}, f32[1,96,768]{2,1,0:T(8,128)S(1)}, u32[]{:S(2)}, u32[]{:S(2)}) collective-permute-start(f32[1,96,768]{2,1,0:T(8,128)S(1)} %slice_add_fusion.7), channel_id=1, source_target_pairs={{0,8},{4,12},{8,0},{12,4},{16,24},{20,28},{24,16},{28,20},{1,9},{5... | collective-permute-start | bytes 884744 | tf_op jit(solution)/shard_map/ppermute | solution.py:196
  549.3 46.6 %collective-permute-start.66 = (f32[1,6,8,768]{3,2,1,0:T(8,128)S(1)}, f32[1,6,8,768]{3,2,1,0:T(8,128)S(1)}, u32[]{:S(2)}, u32[]{:S(2)}) collective-permute-start(f32[1,6,8,768]{3,2,1,0:T(8,128)S(1)} %fusion.156), channel_id=1, source_target_pairs={{0,8},{4,12},{8,0},{12,4},{16,24},{20,28},{24,16},{28,20},{1,9},{5... | collective-permute-start | bytes 442376 | tf_op jit(solution)/shard_map/ppermute | solution.py:196
  549.9 47.4 %collective-permute-start.85 = (f32[2,6,8,768]{3,2,1,0:T(8,128)S(1)}, f32[2,6,8,768]{3,2,1,0:T(8,128)S(1)}, u32[]{:S(2)}, u32[]{:S(2)}) collective-permute-start(f32[2,6,8,768]{3,2,1,0:T(8,128)S(1)} %pad_maximum_fusion.56), channel_id=1, source_target_pairs={{0,8},{4,12},{8,0},{12,4},{16,24},{20,28},{24,16},{28,20},{1,9},{5... | collective-permute-start | bytes 884744 | tf_op jit(solution)/shard_map/ppermute | solution.py:196
  553.7 43.7 %collective-permute-start.120 = (f32[1,1,96,768]{3,2,1,0:T(8,128)S(1)}, f32[1,1,96,768]{3,2,1,0:T(8,128)S(1)}, u32[]{:S(2)}, u32[]{:S(2)}) collective-permute-start(f32[1,1,96,768]{3,2,1,0:T(8,128)S(1)} %fusion.112), channel_id=1, source_target_pairs={{0,16},{4,20},{8,24},{12,28},{16,0},{20,4},{24,8},{28,12},{1,17},{... | collective-permute-start | bytes 884744 | tf_op jit(solution)/shard_map/ppermute | solution.py:196
  561.1 37.4 %collective-permute-start.102 = (f32[1,1,96,768]{3,2,1,0:T(8,128)S(1)}, f32[1,1,96,768]{3,2,1,0:T(8,128)S(1)}, u32[]{:S(2)}, u32[]{:S(2)}) collective-permute-start(f32[1,1,96,768]{3,2,1,0:T(8,128)S(1)} %fusion.124), channel_id=1, source_target_pairs={{0,8},{4,12},{8,0},{12,4},{16,24},{20,28},{24,16},{28,20},{1,9},{5... | collective-permute-start | bytes 884744 | tf_op jit(solution)/shard_map/ppermute | solution.py:196
  561.6 62.7 %collective-permute-start.50 = (f32[512,768]{1,0:T(8,128)}, f32[512,768]{1,0:T(8,128)}, u32[]{:S(2)}, u32[]{:S(2)}) collective-permute-start(f32[512,768]{1,0:T(8,128)} %collective-permute-done.49), channel_id=1, source_target_pairs={{0,1},{1,2},{2,3},{3,0},{4,5},{5,6},{6,7},{7,4},{8,9},{9,10},{10,1... | collective-permute-start | bytes 4718600 | tf_op jit(solution)/shard_map/ppermute | solution.py:200
  (168 other events, 1958.8 us)
